TPU v7x, 128 devices: a whole 4x4x4 slice. The times are simulated.
128 devices in a mesh: row: 8 (over y, core), col: 16 (over x, z).
Axes of the slice: x: 4, y: 4, z: 4, core: 2. Of those that a mesh axis runs over, the one named last changes fastest.
Arguments:
- probes: float32 [131072, 256], P(('row', 'col')), may hold values from -6 to 6
- near_blocks: bfloat16 [128, 8, 1024, 1024], P(('row', 'col')), may hold values from -0.09375 to 0.09375
- near_leaves: int32 [128, 8], P(('row', 'col')), may hold values from 0 to 15, as said below
- near_count: int32 [128], P(('row', 'col')), may hold values from 1 to 8, as said below
- leaf_rank: int32 [128], P(('row', 'col')), may hold values from 128 to 256
- leaf_basis: float32 [131072, 256], P(('row', 'col')), may hold values from -0.1875 to 0.1875
- leaf_transfer: float32 [128, 256, 512], P(('row', 'col')), may hold values from -0.09375 to 0.09375
- leaf_links: int32 [128, 4], P(('row', 'col')), may hold values from 0 to 15, as said below
- leaf_link_blocks: float32 [128, 4, 256, 256], P(('row', 'col')), may hold values from -0.1875 to 0.1875
- parent_links: int32 [8, 2], P('row'), may hold values from 0 to 7, as said below
- parent_link_blocks: float32 [8, 2, 512, 512], P('row'), may hold values from -0.1875 to 0.1875
Outputs:
- term_one: float32 [131072, 256], P(('row', 'col'))
- term_two: float32 [131072, 256], P(('row', 'col'))
Inputs may be any that keep to these rules, and one draw needn't show every extreme that they name: `near_leaves`: slot 0 of every leaf is the leaf's own position; slots 1 to near_count - 1 are distinct other positions of the same group; later slots repeat the leaf's own position. `near_count`: some leaf has 8 live slots in every draw. `leaf_links`: each leaf's 4 coupled positions are distinct and differ from its own. `parent_links`: each parent's 2 coupled parents are distinct and differ from itself.
All inputs are finite; a program needn't handle non-finite values.
Results may differ from a plain program's by a relative error of at most 0.0034.
Values may be sent and summed in bfloat16 or wider, within the bound.
A program may use at most 128 MiB of HBM per device.

v0:
```python
import jax
import jax.numpy as jnp
from jax import lax
from jax.sharding import PartitionSpec as P


def cut_along(value, dim, peers):
    dims = value.shape
    blocks = value.reshape(*dims[:dim], peers, dims[dim] // peers, *dims[dim + 1 :])
    return jnp.moveaxis(blocks, dim, 0)


def sent_and_summed(value, axis, dim):
    blocks = cut_along(value, dim, lax.axis_size(axis))
    arrived = lax.all_to_all(blocks, axis, split_axis=0, concat_axis=0, tiled=True)
    return arrived.sum(axis=0)


def laid_out(blocks, dim):
    blocks = jnp.moveaxis(blocks, 0, dim)
    dims = blocks.shape
    return blocks.reshape(*dims[:dim], dims[dim] * dims[dim + 1], *dims[dim + 2 :])


def from_everyone(value, axis):
    peers = lax.axis_size(axis)
    return lax.all_to_all(
        jnp.broadcast_to(value[None], (peers, *value.shape)), axis, 0, 0, tiled=True
    )


def gather_directly(value, axis, dim):
    return laid_out(from_everyone(value, axis), dim)


def local(
    probes,
    near_blocks,
    near_leaves,
    near_count,
    leaf_rank,
    leaf_basis,
    leaf_transfer,
    leaf_links,
    leaf_link_blocks,
    parent_links,
    parent_link_blocks,
):
    highest = lax.Precision.HIGHEST
    span_col = lax.axis_size("col")
    span_row = lax.axis_size("row")
    leaf_rows = probes.shape[0]
    probe_cols = probes.shape[1]
    rank_cols = leaf_basis.shape[1]
    parent_cols = leaf_transfer.shape[2]
    rank_mask = (jnp.arange(rank_cols, dtype=jnp.int32) < leaf_rank[0]).astype(jnp.float32)[:, None]
    transfer = leaf_transfer[0]
    own_blocks = near_blocks[0]
    own_near = near_leaves[0]

    def multiply(vector):
        packed = vector.astype(jnp.bfloat16)
        empty = jnp.zeros((leaf_rows, probe_cols), jnp.float32)
        stacked = lax.all_gather(packed, "col", axis=0, tiled=True).reshape(
            span_col, leaf_rows, probe_cols
        )

        def add_slot(slot, total):
            near_block = lax.dynamic_index_in_dim(own_blocks, slot, 0, False)
            source = lax.dynamic_index_in_dim(stacked, own_near[slot], 0, False)
            return total + jnp.dot(near_block, source, preferred_element_type=jnp.float32)

        near_sum = lax.fori_loop(0, near_count[0], add_slot, empty)
        skeleton = jnp.dot(leaf_basis.T, vector, precision=highest) * rank_mask
        gathered = lax.all_gather(skeleton, "col", axis=0, tiled=True).reshape(
            span_col, rank_cols, probe_cols
        )
        linked = gathered[leaf_links[0]]
        coupled = jnp.einsum("kab,kbp->ap", leaf_link_blocks[0], linked, precision=highest)
        upward = jnp.dot(transfer.T, skeleton, precision=highest)
        portion = sent_and_summed(upward, "col", 1)
        every_parent = gather_directly(portion, "row", 0).reshape(span_row, parent_cols, -1)
        far_portion = jnp.einsum(
            "kab,kbp->ap", parent_link_blocks[0], every_parent[parent_links[0]], precision=highest
        )
        far_parent = gather_directly(far_portion, "col", 1)
        combined = (coupled + jnp.dot(transfer, far_parent, precision=highest)) * rank_mask
        return jnp.dot(leaf_basis, combined, precision=highest) + near_sum

    term_one = multiply(probes)
    term_two = 2.0 * multiply(term_one) - probes
    return (term_one, term_two)


def solution(mesh):
    in_specs = (
        P(("row", "col"), None),
        P(("row", "col"), None, None, None),
        P(("row", "col"), None),
        P(("row", "col")),
        P(("row", "col")),
        P(("row", "col"), None),
        P(("row", "col"), None, None),
        P(("row", "col"), None),
        P(("row", "col"), None, None, None),
        P("row", None),
        P("row", None, None, None),
    )
    out_specs = (P(("row", "col"), None), P(("row", "col"), None))
    return jax.shard_map(local, mesh=mesh, in_specs=in_specs, out_specs=out_specs, check_vma=False)
```

profile of v0, /device:TPU:0, one launch (start us, length us, event | category | flops | bytes accessed | tf_op | source)
XLA Modules:
  0.0 398.8 jit_solution(15930969842842433636)
XLA Ops:
  8.1 4.1 %convolution_multiply_fusion.1 = f32[256,256]{1,0:T(8,128)} fusion(f32[1024,256]{1,0:T(8,128)} %param.20, f32[1024,256]{1,0:T(8,128)} %param.15, f32[256]{0:T(256)S(1)} %compare_convert_fusion), kind=kOutput, calls=%fused_computation.35 | convolution fusion | flops 805371904 | bytes 2360320 | tf_op jit(solution)/shard_map/dot_general | solution.py:74
  12.2 2.1 convert_element_type.14
  14.3 2.4 fusion.40
  16.7 8.0 %all-to-all-start = ((f32[16,512,16]{1,2,0:T(8,128)}), f32[16,512,16]{1,2,0:T(8,128)S(1)}, u32[]{:S(2)}, u32[]{:S(2)}) async-start(f32[16,512,16]{1,2,0:T(8,128)} %bitcast.131), calls=%async_computation | async-start | bytes 1048576 | tf_op jit(solution)/shard_map/all_to_all | solution.py:15
  24.7 14.3 %all-to-all-done = f32[16,512,16]{1,2,0:T(8,128)S(1)} async-done(((f32[16,512,16]{1,2,0:T(8,128)}), f32[16,512,16]{1,2,0:T(8,128)S(1)}, u32[]{:S(2)}, u32[]{:S(2)}) %all-to-all-start) | async-done | bytes 524320 | tf_op jit(solution)/shard_map/all_to_all | solution.py:15
  39.8 4.7 %all-to-all-start.1 = ((f32[8,512,16]{1,2,0:T(8,128)}), f32[8,512,16]{1,2,0:T(8,128)S(1)}, u32[]{:S(2)}, u32[]{:S(2)}) async-start(f32[8,512,16]{1,2,0:T(8,128)} %broadcast_in_dim.8), calls=%async_computation.1 | async-start | bytes 524288 | tf_op jit(solution)/shard_map/all_to_all | solution.py:27
  44.4 7.5 %all-to-all-done.1 = f32[8,512,16]{1,2,0:T(8,128)S(1)} async-done(((f32[8,512,16]{1,2,0:T(8,128)}), f32[8,512,16]{1,2,0:T(8,128)S(1)}, u32[]{:S(2)}, u32[]{:S(2)}) %all-to-all-start.1) | async-done | bytes 262176 | tf_op jit(solution)/shard_map/all_to_all | solution.py:27
  52.5 1.8 fusion.28
  55.3 3.7 all-to-all-start.2
  59.1 16.6 %all-gather.5.cloned.1.call-done = f32[4096,256]{1,0:T(8,128)} async-done(((f32[256,256]{1,0:T(8,128)}), f32[4096,256]{1,0:T(8,128)}) %all-gather.5.cloned.1.call-update) | async-done | bytes 4194320 | tf_op jit(solution)/shard_map/all_gather | solution.py:75
  75.7 3.8 gather_fusion
  79.5 3.4 convolution_bitcast_fusion.3
  82.9 1.3 fusion.26
  84.2 64.7 %all-gather.7.cloned.1.call-done = bf16[16384,256]{1,0:T(8,128)(2,1)} async-done(((bf16[1024,256]{1,0:T(8,128)(2,1)}), bf16[16384,256]{1,0:T(8,128)(2,1)}) %all-gather.7.cloned.1.call-update) | async-done | bytes 8388624 | tf_op jit(solution)/shard_map/all_gather | solution.py:64
  149.0 40.0 %while.20 = (s32[]{:T(128)}, f32[1024,256]{1,0:T(8,128)S(1)}, s32[]{:T(128)}, bf16[8,1024,1024]{2,1,0:T(8,128)(2,1)}, s32[8]{0:T(128)S(1)}, /*index=5*/bf16[16,1...) while((s32[]{:T(128)}, f32[1024,256]{1,0:T(8,128)S(1)}, s32[]{:T(128)}, ...), condition=%wide.region_2.3_spmd, body=%wide.region_1.2_spmd.sunk | while | flops 537133056 | bytes 4718781 | solution.py:73
  152.2 2.4 fusion.69
  157.9 2.4 fusion.69
  163.5 2.4 fusion.69
  169.1 2.4 fusion.69
  174.7 2.4 fusion.69
  180.3 2.4 fusion.69
  186.0 2.4 fusion.69
  189.0 1.3 copy.21
  190.3 3.5 fusion.44
  193.9 1.7 convolution_multiply_fusion
  196.2 1.8 fusion.37
  198.0 22.7 %all_to_all.31 = f32[16,512,16]{1,2,0:T(8,128)} all-to-all(f32[16,512,16]{1,2,0:T(8,128)S(1)} %bitcast.132), channel_id=1, replica_groups=mesh['row'=8,'col'=16] {'col'}, dimensions={0} | all-to-all | bytes 1048576 | tf_op jit(solution)/shard_map/all_to_all | solution.py:15
  221.9 10.9 %all_to_all.30 = f32[8,512,16]{1,2,0:T(8,128)S(1)} all-to-all(f32[8,512,16]{1,2,0:T(8,128)S(1)} %broadcast_in_dim.10), channel_id=1, replica_groups=mesh['row'=8,'col'=16] {'row'}, dimensions={0} | all-to-all | bytes 524288 | tf_op jit(solution)/shard_map/all_to_all | solution.py:27
  233.3 1.8 fusion.31
  236.0 3.9 all-to-all-start.5
  239.9 1.3 copy.25
  242.5 21.4 %all-gather.9.cloned.1.call-done = f32[4096,256]{0,1:T(8,128)} async-done(((f32[256,256]{0,1:T(8,128)}), f32[4096,256]{0,1:T(8,128)}) %all-gather.9.cloned.1.call-update) | async-done | bytes 4194320 | tf_op jit(solution)/shard_map/all_gather | solution.py:75
  263.9 5.6 %copy.28 = f32[4096,256]{1,0:T(8,128)} copy(f32[4096,256]{0,1:T(8,128)} %all-gather.9.cloned.1.call-done) | data formatting | bytes 8388608 | tf_op jit(solution)/shard_map/reshape | solution.py:75
  269.5 2.9 gather_fusion.2
  272.4 2.5 convolution_bitcast_fusion.2
  274.9 1.6 fusion.27
  276.5 58.7 %all-gather.11.cloned.1.call-done = bf16[16384,256]{0,1:T(8,128)(2,1)} async-done(((bf16[1024,256]{0,1:T(8,128)(2,1)}), bf16[16384,256]{0,1:T(8,128)(2,1)}) %all-gather.11.cloned.1.call-update) | async-done | bytes 8388624 | tf_op jit(solution)/shard_map/all_gather | solution.py:64
  335.2 11.4 %copy.29 = bf16[16384,256]{1,0:T(8,128)(2,1)} copy(bf16[16384,256]{0,1:T(8,128)(2,1)} %all-gather.11.cloned.1.call-done) | data formatting | bytes 16777216 | tf_op jit(solution)/shard_map/while | solution.py:73
  346.7 40.0 %while.21 = (s32[]{:T(128)}, f32[1024,256]{1,0:T(8,128)S(1)}, s32[]{:T(128)}, bf16[8,1024,1024]{2,1,0:T(8,128)(2,1)}, s32[8]{0:T(128)S(1)}, /*index=5*/bf16[16,1...) while((s32[]{:T(128)}, f32[1024,256]{1,0:T(8,128)S(1)}, s32[]{:T(128)}, ...), condition=%wide.region_5.6_spmd, body=%wide.region_4.5_spmd.sunk | while | flops 537133056 | bytes 4718781 | solution.py:73
  349.9 2.4 fusion.72
  355.5 2.4 fusion.72
  361.1 2.4 fusion.72
  366.7 2.4 fusion.72
  372.4 2.4 fusion.72
  378.0 2.4 fusion.72
  383.6 2.4 fusion.72
  386.7 1.3 copy.24
  388.0 2.9 fusion.25
  (67 shorter events, 16.6 us)
Async XLA Ops:
  7.2 45.4 %copy-start = (f32[1,2,512,512]{3,2,1,0:T(8,128)S(1)}, f32[1,2,512,512]{3,2,1,0:T(8,128)}, u32[]{:S(2)}) copy-start(f32[1,2,512,512]{3,2,1,0:T(8,128)} %param.25) | copy-start | bytes 6291460
  7.2 7.1 %copy-start.6 = (f32[1,256,512]{2,1,0:T(8,128)S(1)}, f32[1,256,512]{2,1,0:T(8,128)}, u32[]{:S(2)}) copy-start(f32[1,256,512]{2,1,0:T(8,128)} %param.21) | copy-start | bytes 1572868
  7.2 68.5 %all-gather.5.cloned.1.call-start = ((), (), s32[]{:S(2)}) async-start(), calls=%async_computation.6 | async-start | bytes 4456448 | tf_op jit(solution)/shard_map/all_gather | solution.py:75
  8.1 36.3 %copy-start.10 = (s32[1,2]{1,0:T(1,128)S(1)}, s32[1,2]{1,0:T(1,128)}, u32[]{:S(2)}) copy-start(s32[1,2]{1,0:T(1,128)} %param.24) | copy-start | bytes 28
  12.2 136.7 %all-gather.7.cloned.1.call-start = ((), (), s32[]{:S(2)}) async-start(), calls=%async_computation.7 | async-start | bytes 8912896 | tf_op jit(solution)/shard_map/all_gather | solution.py:64
  14.3 44.7 %copy-start.11 = (s32[1,4]{1,0:T(1,128)S(1)}, s32[1,4]{1,0:T(1,128)}, u32[]{:S(2)}) copy-start(s32[1,4]{1,0:T(1,128)} %param.22) | copy-start | bytes 52
  16.7 22.3 %all-to-all-start = ((f32[16,512,16]{1,2,0:T(8,128)}), f32[16,512,16]{1,2,0:T(8,128)S(1)}, u32[]{:S(2)}, u32[]{:S(2)}) async-start(f32[16,512,16]{1,2,0:T(8,128)} %bitcast.131), calls=%async_computation | async-start | bytes 1048576 | tf_op jit(solution)/shard_map/all_to_all | solution.py:15
  39.8 12.2 %all-to-all-start.1 = ((f32[8,512,16]{1,2,0:T(8,128)}), f32[8,512,16]{1,2,0:T(8,128)S(1)}, u32[]{:S(2)}, u32[]{:S(2)}) async-start(f32[8,512,16]{1,2,0:T(8,128)} %broadcast_in_dim.8), calls=%async_computation.1 | async-start | bytes 524288 | tf_op jit(solution)/shard_map/all_to_all | solution.py:27
  55.3 93.7 %copy-start.12 = (s32[1,8]{1,0:T(1,128)S(1)}, s32[1,8]{1,0:T(1,128)}, u32[]{:S(2)}) copy-start(s32[1,8]{1,0:T(1,128)} %param.17) | copy-start | bytes 100
  55.3 27.6 %all-to-all-start.2 = ((f32[16,512,16]{1,2,0:T(8,128)}), f32[16,512,16]{1,2,0:T(8,128)S(1)}, u32[]{:S(2)}, u32[]{:S(2)}) async-start(f32[16,512,16]{1,2,0:T(8,128)} %broadcast_in_dim.9), calls=%async_computation.2 | async-start | bytes 1048576 | tf_op jit(solution)/shard_map/all_to_all | solution.py:27
  59.0 204.9 %all-gather.9.cloned.1.call-start = ((), (), s32[]{:S(2)}) async-start(), calls=%async_computation.8 | async-start | bytes 4456448 | tf_op jit(solution)/shard_map/all_gather | solution.py:75
  149.0 41.4 %copy-start.9 = (f32[256,256]{1,0:T(8,128)S(1)}, f32[256,256]{1,0:T(8,128)}, u32[]{:S(2)}) copy-start(f32[256,256]{1,0:T(8,128)} %fusion.26) | copy-start | bytes 786436
  190.3 3.5 copy-start.2
  193.8 1.7 copy-start.4
  195.6 139.6 %all-gather.11.cloned.1.call-start = ((), (), s32[]{:S(2)}) async-start(), calls=%async_computation.9 | async-start | bytes 8912896 | tf_op jit(solution)/shard_map/all_gather | solution.py:64
  196.2 43.7 %copy-start.3 = (f32[1024,256]{1,0:T(8,128)S(1)}, f32[1024,256]{1,0:T(8,128)}, u32[]{:S(2)}) copy-start(f32[1024,256]{1,0:T(8,128)} %param.15) | copy-start | bytes 3145732
  235.1 6.1 %copy-start.5 = (f32[1024,256]{0,1:T(8,128)S(1)}, f32[1024,256]{0,1:T(8,128)}, u32[]{:S(2)}) copy-start(f32[1024,256]{0,1:T(8,128)} %copy-done.4) | copy-start | bytes 3145732
  236.0 39.0 %all-to-all-start.5 = ((f32[16,512,16]{1,2,0:T(8,128)}), f32[16,512,16]{1,2,0:T(8,128)S(1)}, u32[]{:S(2)}, u32[]{:S(2)}) async-start(f32[16,512,16]{1,2,0:T(8,128)} %broadcast_in_dim.11), calls=%async_computation.5 | async-start | bytes 1048576 | tf_op jit(solution)/shard_map/all_to_all | solution.py:27
  242.5 29.9 %copy-start.8 = (f32[1,4,256,256]{3,2,1,0:T(8,128)S(1)}, f32[1,4,256,256]{3,2,1,0:T(8,128)}, u32[]{:S(2)}) copy-start(f32[1,4,256,256]{3,2,1,0:T(8,128)} %param.23) | copy-start | bytes 3145732
  269.5 5.4 %copy-start.7 = (f32[1,256,512]{2,1,0:T(8,128)S(1)}, f32[1,256,512]{2,1,0:T(8,128)}, u32[]{:S(2)}) copy-start(f32[1,256,512]{2,1,0:T(8,128)} %param.21) | copy-start | bytes 1572868
  386.7 5.6 %copy-start.1 = (f32[1,2,512,512]{3,2,1,0:T(8,128)S(1)}, f32[1,2,512,512]{3,2,1,0:T(8,128)}, u32[]{:S(2)}) copy-start(f32[1,2,512,512]{3,2,1,0:T(8,128)} %param.25) | copy-start | bytes 6291460
Sparse Core Ops, SparseCore 0:
  12.3 63.3 all-gather.4
  78.4 70.4 all-gather.6
  195.7 68.1 all-gather.8
  266.0 69.2 all-gather.10
where the time goes:
time: 407 us; the launch traced here: 399 us
  waiting for transfers between devices  184 us (45%)
  matrix products  62.7 us (15%)
  local copies, waits for them, and re-layouts  42.3 us (10%)
  loops' own time  38 us (9%)
  blocking collectives  33.6 us (8%)
  starting transfers between devices  20.4 us (5%)
  between operations  14.9 us (4%)
    all_gather x2, waiting for transfers between devices, multiply(): lax.all_gather(packed, 'col', axis=0, tiled=True)  123 us
    all_gather x2, waiting for transfers between devices, multiply(): lax.all_gather(skeleton, 'col', axis=0, tiled=True)  38 us
    another operation x2, loops' own time, multiply(): near_sum = lax.fori_loop(0, near_count[0], add_slot, empty)  38 us
    dot_general x14, matrix products, add_slot(): jnp.dot(near_block, source, preferred_element_type=jnp.float32)  33.8 us
    all_to_all x1, blocking collectives, sent_and_summed(): lax.all_to_all(blocks, axis, split_axis=0, concat_axis=0, tiled=True)  22.7 us
    all_to_all x1, waiting for transfers between devices, sent_and_summed(): lax.all_to_all(blocks, axis, split_axis=0, concat_axis=0, tiled=True)  14.3 us
    while x3, local copies, waits for them, and re-layouts, multiply(): near_sum = lax.fori_loop(0, near_count[0], add_slot, empty)  14 us
    all_to_all x3, starting transfers between devices, from_everyone(): lax.all_to_all(jnp.broadcast_to(value[None], (peers, *value.shape)), axis...  12.3 us
  transfers between devices with their start and end apart: 8, of which 6 were waited for; matrix products, arithmetic and copies ran while one was open for 10% of the time, Pallas kernels for 0%

commit v1 on v0

v1 whole, which is shorter than its diff:
```python
import functools

import jax
import jax.numpy as jnp
from jax import lax
from jax.experimental import pallas as pl
from jax.experimental.pallas import tpu as pltpu
from jax.sharding import PartitionSpec as P

BF = jnp.bfloat16
F32 = jnp.float32
SIDE = 4
PEERS = SIDE * SIDE
LEAF = 1024
HALF = LEAF // 2
RANK = 256
PARENT = 512
PROBES = 256
CHUNKS = 2
COLS = PROBES // CHUNKS
STAGES = 2 * CHUNKS
BLOCK = HALF + RANK // 2
PIECE = BLOCK // 2
SHARE = PROBES // CHUNKS // PEERS


def dot(a, b, ca=1, cb=0):
    return lax.dot_general(a, b, (((ca,), (cb,)), ((), ())), preferred_element_type=F32)


def split(value):
    high = value.astype(BF)
    return high, (value - high.astype(F32)).astype(BF)


def dot_split(ah, al, bh, bl):
    return dot(ah, bh) + (dot(al, bh) + dot(ah, bl))


def fold(value):
    return jnp.concatenate([value[:, : PARENT // 2], value[:, PARENT // 2 :]], axis=0)


def unfold(value):
    return jnp.concatenate([value[:SHARE], value[SHARE:]], axis=1)


def kernel(
    rows,
    near_leaves, near_count, leaf_rank, leaf_links, parent_links,
    probes, near, basis, transfer, link_blocks, parent_blocks,
    out_one, out_two,
    g, near_buf, v_buf, acc, coup, t_buf,
    basis_f, transfer_f, link_f, parent_f,
    u_hi, u_lo, ut_hi, ut_lo, e_bf, l_bf, b_bf,
    up_send, up_recv, par, far_recv,
    near_slot, near_has, link_slot, link_has,
    load_sem, out_sem, g_send, g_recv, up_ss, up_rs, row_ss, row_rs, far_ss, far_rs,
):
    row = lax.axis_index("row")
    me = lax.axis_index("col")
    x, z = me // SIDE, me % SIDE

    loads = [
        pltpu.make_async_copy(src, dst, load_sem.at[i])
        for i, (src, dst) in enumerate(
            (
                (probes, v_buf),
                (basis, basis_f),
                (transfer.at[0], transfer_f),
                (link_blocks.at[0], link_f),
                (parent_blocks.at[0], parent_f),
                (near.at[0], near_buf),
            )
        )
    ]
    for load in loads:
        load.start()

    barrier = pltpu.get_barrier_semaphore()
    for d in range(1, PEERS):
        pl.semaphore_signal(barrier, inc=1, device_id={"col": (me + d) % PEERS})
    for d in range(1, rows):
        pl.semaphore_signal(barrier, inc=1, device_id={"row": (row + d) % rows})

    count = near_count[0]
    for a in range(SIDE):
        for b in range(SIDE):
            source = ((x + SIDE - a) % SIDE) * SIDE + (z + SIDE - b) % SIDE
            slot, has = jnp.int32(0), jnp.int32(0)
            for k in range(8):
                hit = jnp.logical_and(near_leaves[0, k] == source, k < count)
                slot, has = jnp.where(hit, k, slot), jnp.where(hit, 1, has)
            near_slot[a * SIDE + b] = slot
            near_has[a * SIDE + b] = has
            slot, has = jnp.int32(0), jnp.int32(0)
            for k in range(4):
                hit = leaf_links[0, k] == source
                slot, has = jnp.where(hit, k, slot), jnp.where(hit, 1, has)
            link_slot[a * SIDE + b] = slot
            link_has[a * SIDE + b] = has

    rank = leaf_rank[0]
    mask = lax.broadcasted_iota(jnp.int32, (RANK, COLS), 0) < rank

    def masked(value):
        return jnp.where(mask, value, jnp.zeros_like(value))

    def slot_of(half, p, q):
        return p * SIDE + q if half == 0 else q * SIDE + p

    def at_step(half, first, step):
        along_x = first == (half == 0)
        if along_x:
            return {"col": ((x + step + SIDE) % SIDE) * SIDE + z}
        return {"col": x * SIDE + (z + step + SIDE) % SIDE}

    def send(s, half, source, target, first, step, piece=None):
        src, dst = g.at[s, half, source], g.at[s, half, target]
        if piece is not None:
            part = pl.ds(piece * PIECE, PIECE)
            src, dst = src.at[part], dst.at[part]
        pltpu.make_async_remote_copy(
            src_ref=src,
            dst_ref=dst,
            send_sem=g_send.at[s, half],
            recv_sem=g_recv.at[s, half, target],
            device_id=at_step(half, first, step),
        ).start()

    def along_first(s, half, step, piece=None):
        source = slot_of(half, 0, 0) if piece is None else slot_of(half, step % SIDE, 0)
        target = slot_of(half, (step if piece is None else 2) % SIDE, 0)
        send(s, half, source, target, True, step, piece)

    def along_second(s, half, p, step, piece=None):
        source = slot_of(half, p, 0 if piece is None else step % SIDE)
        target = slot_of(half, p, (step if piece is None else 2) % SIDE)
        send(s, half, source, target, False, step, piece)

    def send_own(s):
        for half in range(2):
            for step in (1, -1):
                along_first(s, half, step)
            for step in (1, -1):
                along_second(s, half, 0, step)

    def arrive(s, half, p, q):
        slot = slot_of(half, p, q)
        ref = g.at[s, half, slot]
        pltpu.make_async_copy(ref, ref, g_recv.at[s, half, slot]).wait()
        if q == 0:
            if p == 1:
                along_first(s, half, 1, 0)
            if p == 3:
                along_first(s, half, -1, 1)
            along_second(s, half, p, 1)
            along_second(s, half, p, -1)
        elif q == 1:
            along_second(s, half, p, 1, 0)
        elif q == 3:
            along_second(s, half, p, -1, 1)

    def product(s, half, slot):
        block = g[s, half, slot, :HALF]
        block = jnp.where(near_has[slot] > 0, block, jnp.zeros_like(block))
        acc[...] += dot(near_buf[near_slot[slot], :, half * HALF : (half + 1) * HALF], block)
        block = g[s, half, slot, HALF:]
        block = jnp.where(link_has[slot] > 0, block, jnp.zeros_like(block))
        width = RANK // 2
        coup[...] += dot(l_bf[link_slot[slot], :, half * width : (half + 1) * width], block)

    def make_message(s, v):
        high, low = split(v)
        skeleton = masked(dot_split(ut_hi[...], ut_lo[...], high, low))
        packed = skeleton.astype(BF)
        for half in range(2):
            g[s, half, 0, :HALF] = high[half * HALF : (half + 1) * HALF]
            g[s, half, 0, HALF:] = packed[half * RANK // 2 : (half + 1) * RANK // 2]
        return skeleton

    def to_peers(src_of, dst_of, ss, rs):
        for d in range(1, PEERS):
            peer = (me + d) % PEERS
            pltpu.make_async_remote_copy(
                src_ref=src_of(peer), dst_ref=dst_of(d), send_sem=ss, recv_sem=rs, device_id={"col": peer}
            ).start()

    def upward(s, skeleton):
        up = dot(skeleton.T.astype(BF), e_bf[...])
        for j in range(PEERS):
            up_send[s, j] = fold(up[j * SHARE : (j + 1) * SHARE]).astype(BF)
        up_recv[s, 0] = up_send[s, me]
        to_peers(
            lambda peer: up_send.at[s, peer], lambda d: up_recv.at[s, d], up_ss.at[s], up_rs.at[s]
        )

    def wait_all(ref, sem):
        pltpu.make_async_copy(ref, ref, sem).wait()

    def parents(s):
        wait_all(up_recv.at[s, pl.ds(1, PEERS - 1)], up_rs.at[s])
        total = up_recv[s, 0].astype(F32)
        for d in range(1, PEERS):
            total += up_recv[s, d].astype(F32)
        par[s, 0] = total.astype(BF)
        for d in range(1, rows):
            pltpu.make_async_remote_copy(
                src_ref=par.at[s, 0],
                dst_ref=par.at[s, d],
                send_sem=row_ss.at[s],
                recv_sem=row_rs.at[s],
                device_id={"row": (row + d) % rows},
            ).start()

    def far(s):
        wait_all(par.at[s, pl.ds(1, rows - 1)], row_rs.at[s])
        total = jnp.zeros((SHARE, PARENT), F32)
        for k in range(2):
            away = (row + rows - parent_links[0, k]) % rows
            source = jnp.zeros((2 * SHARE, PARENT // 2), F32)
            for d in range(1, rows):
                source = jnp.where(away == d, par[s, d].astype(F32), source)
            source = source.astype(BF)
            total += dot(source, b_bf[k, :, : PARENT // 2], 1, 1)[:SHARE]
            total += dot(source, b_bf[k, :, PARENT // 2 :], 1, 1)[SHARE:]
        far_recv[s, me] = fold(total).astype(BF)
        to_peers(
            lambda peer: far_recv.at[s, me], lambda d: far_recv.at[s, me], far_ss.at[s], far_rs.at[s]
        )

    def combined_result(s):
        wait_all(far_recv.at[s, pl.ds(0, PEERS - 1)], far_rs.at[s])
        far_parent = jnp.concatenate(
            [unfold(far_recv[s, j].astype(F32)) for j in range(PEERS)], axis=0
        ).astype(BF)
        high, low = split(masked(coup[...] + dot(e_bf[...], far_parent, 1, 1)))
        return dot_split(u_hi[...], u_lo[...], high, low) + acc[...]

    loads[0].wait()
    loads[1].wait()
    u = basis_f[...]
    u_hi[...], u_lo[...] = split(u)
    ut_hi[...], ut_lo[...] = split(u.T)
    pl.semaphore_wait(barrier, PEERS - 1 + rows - 1)
    first = make_message(0, v_buf[:, :COLS])
    send_own(0)
    loads[2].wait()
    e_bf[...] = transfer_f[...].astype(BF)
    upward(0, first)
    for c in range(1, CHUNKS):
        upward(c, make_message(c, v_buf[:, c * COLS : (c + 1) * COLS]))
    loads[3].wait()
    l_bf[...] = link_f[...].astype(BF)
    loads[4].wait()
    b_bf[...] = parent_f[...].astype(BF)
    loads[5].wait()

    events = [(1, 0), (3, 0), (0, 1), (0, 3), (2, 0)]
    events += [(p, q) for p in (1, 3, 2) for q in (1, 3)]
    events += [(0, 2), (1, 2), (3, 2), (2, 2)]
    events = [(half, p, q) for p, q in events for half in range(2)]

    @pl.loop(0, STAGES)
    def _(s):
        acc[...] = jnp.zeros_like(acc)
        coup[...] = jnp.zeros_like(coup)
        columns = pl.ds(pl.multiple_of((s % CHUNKS) * COLS, COLS), COLS)
        for half in range(2):
            product(s, half, 0)
        for i, (half, p, q) in enumerate(events):
            arrive(s, half, p, q)
            product(s, half, slot_of(half, p, q))
            if i == 5:
                pl.when(s == 0)(lambda: parents(0))
            if i == 9:
                pl.when(s == 0)(lambda: far(0))
            if i == 7:
                pl.when(s + 1 < STAGES)(lambda: parents(s + 1))
            if i == 15:
                pl.when(s + 1 < STAGES)(lambda: far(s + 1))
            if i == 17:
                pl.when(s + 1 < STAGES)(lambda: send_own(s + 1))

        t_buf[s] = combined_result(s)

        @pl.when(s < CHUNKS)
        def _():
            pltpu.make_async_copy(t_buf.at[s], out_one.at[:, columns], out_sem.at[s]).start()
            skeleton = make_message(s + CHUNKS, t_buf[s])
            upward(s + CHUNKS, skeleton)

        @pl.when(s >= CHUNKS)
        def _():
            t_buf[s] = 2.0 * t_buf[s] - v_buf[:, columns]
            pltpu.make_async_copy(t_buf.at[s], out_two.at[:, columns], out_sem.at[s]).start()

    for s in range(STAGES):
        columns = pl.ds((s % CHUNKS) * COLS, COLS)
        out = out_one if s < CHUNKS else out_two
        for half in range(2):
            wait_all(g.at[s, half, pl.ds(0, PEERS - 1)], g_send.at[s, half])
        wait_all(up_recv.at[s, pl.ds(1, PEERS - 1)], up_ss.at[s])
        wait_all(par.at[s, pl.ds(1, rows - 1)], row_ss.at[s])
        wait_all(far_recv.at[s, pl.ds(1, PEERS - 1)], far_ss.at[s])
        pltpu.make_async_copy(t_buf.at[s], out.at[:, columns], out_sem.at[s]).wait()


def local(
    probes,
    near_blocks,
    near_leaves,
    near_count,
    leaf_rank,
    leaf_basis,
    leaf_transfer,
    leaf_links,
    leaf_link_blocks,
    parent_links,
    parent_link_blocks,
):
    rows = lax.axis_size("row")
    smem = pl.BlockSpec(memory_space=pltpu.SMEM)
    hbm = pl.BlockSpec(memory_space=pl.ANY)
    dma = pltpu.SemaphoreType.DMA
    vmem = pltpu.VMEM
    folded = (2 * SHARE, PARENT // 2)
    return pl.pallas_call(
        functools.partial(kernel, rows),
        out_shape=[jax.ShapeDtypeStruct((LEAF, PROBES), F32)] * 2,
        in_specs=[smem] * 5 + [hbm] * 6,
        out_specs=[hbm] * 2,
        scratch_shapes=[
            vmem((STAGES, 2, PEERS, BLOCK, COLS), BF),
            vmem((8, LEAF, LEAF), BF),
            vmem((LEAF, PROBES), F32),
            vmem((LEAF, COLS), F32),
            vmem((RANK, COLS), F32),
            vmem((STAGES, LEAF, COLS), F32),
            vmem((LEAF, RANK), F32),
            vmem((RANK, PARENT), F32),
            vmem((4, RANK, RANK), F32),
            vmem((2, PARENT, PARENT), F32),
            vmem((LEAF, RANK), BF),
            vmem((LEAF, RANK), BF),
            vmem((RANK, LEAF), BF),
            vmem((RANK, LEAF), BF),
            vmem((RANK, PARENT), BF),
            vmem((4, RANK, RANK), BF),
            vmem((2, PARENT, PARENT), BF),
            vmem((STAGES, PEERS, *folded), BF),
            vmem((STAGES, PEERS, *folded), BF),
            vmem((STAGES, rows, *folded), BF),
            vmem((STAGES, PEERS, *folded), BF),
            *[pltpu.SMEM((PEERS,), jnp.int32)] * 4,
            dma((6,)),
            dma((STAGES,)),
            dma((STAGES, 2)),
            dma((STAGES, 2, PEERS)),
            *[dma((STAGES,))] * 6,
        ],
        compiler_params=pltpu.CompilerParams(
            collective_id=0, has_side_effects=True, vmem_limit_bytes=62 * 2**20
        ),
    )(
        near_leaves, near_count, leaf_rank, leaf_links, parent_links,
        probes, near_blocks, leaf_basis, leaf_transfer, leaf_link_blocks, parent_link_blocks,
    )


def solution(mesh):
    in_specs = (
        P(("row", "col"), None),
        P(("row", "col"), None, None, None),
        P(("row", "col"), None),
        P(("row", "col")),
        P(("row", "col")),
        P(("row", "col"), None),
        P(("row", "col"), None, None),
        P(("row", "col"), None),
        P(("row", "col"), None, None, None),
        P("row", None),
        P("row", None, None, None),
    )
    out_specs = (P(("row", "col"), None), P(("row", "col"), None))
    return jax.shard_map(local, mesh=mesh, in_specs=in_specs, out_specs=out_specs, check_vma=False)
```

time: 407 us -> 158 us (0.39); the launches traced: 399 us -> 158 us
  waiting for transfers between devices: 184 us -> 0 us
  Pallas kernels: 0 us -> 152 us
  matrix products: 62.7 us -> 0 us
  loops' own time: 38 us -> 0 us
  local copies, waits for them, and re-layouts: 42.3 us -> 4.52 us
  blocking collectives: 33.6 us -> 0 us
  starting transfers between devices: 20.4 us -> 0 us
  between operations: 14.9 us -> 1.93 us
    all_gather x4 -> x0, waiting for transfers between devices: 161 us -> none  [the longest x2 123 us: multiply(): lax.all_gather(packed, 'col', axis=0, tiled=True)]
    pallas_call x0 -> x1, Pallas kernels: none -> 152 us  [local(): pl.pallas_call(functools.partial(kernel, rows), out_shape=[jax.ShapeDtype...]
    dot_general x26 -> x0, matrix products: 62.7 us -> none  [the longest x14 33.8 us: add_slot(): jnp.dot(near_block, source, preferred_element_type=jnp.float32)]
    another operation x2 -> x0, loops' own time: 38 us -> none  [multiply(): near_sum = lax.fori_loop(0, near_count[0], add_slot, empty)]
    all_to_all x2 -> x0, blocking collectives: 33.6 us -> none  [the longest x1 22.7 us: sent_and_summed(): lax.all_to_all(blocks, axis, split_axis=0, concat_axis=0, tiled=True)]
    all_to_all x4 -> x0, waiting for transfers between devices: 21.8 us -> none  [the longest x1 14.3 us: sent_and_summed(): lax.all_to_all(blocks, axis, split_axis=0, concat_axis=0, tiled=True)]
    all_to_all x4 -> x0, starting transfers between devices: 20.2 us -> none  [the longest x3 12.3 us: from_everyone(): lax.all_to_all(jnp.broadcast_to(value[None], (peers, *value.shape)), axis...]
    while x3 -> x0, local copies, waits for them, and re-layouts: 14 us -> none  [multiply(): near_sum = lax.fori_loop(0, near_count[0], add_slot, empty)]
  transfers between devices with their start and end apart: 8 -> 0, of which waited for: 6 -> 0; matrix products, arithmetic and copies ran while one was open for 10% -> 0% of each run, Pallas kernels for 0% -> 0%
where the time goes in v1:
time: 158 us
  Pallas kernels  152 us (96%)
  local copies, waits for them, and re-layouts  4.52 us (3%)
  between operations  1.93 us (1%)
    pallas_call x1, Pallas kernels, local(): pl.pallas_call(functools.partial(kernel, rows), out_shape=[jax.ShapeDtype...  152 us
    unnamed x2, local copies, waits for them, and re-layouts  4.52 us

profile of v1, /device:TPU:0, one launch (start us, length us, event | category | flops | bytes accessed | tf_op | source)
XLA Modules:
  0.0 158.2 jit_solution(3700524082074155850)
XLA Ops:
  1.9 151.7 %shard_map.122 = (f32[1024,256]{1,0:T(8,128)}, f32[1024,256]{1,0:T(8,128)}) custom-call(s32[1,8]{1,0:T(1,128)} %near_leaves.1, s32[1]{0:T(128)S(6)} %copy.15.near_count, s32[1]{0:T(128)S(6)} %copy.16.leaf_rank, s32[1,4]{1,0:T(1,128)} %leaf_links.1, s32[1,2]{1,0:T(1,128)} %parent_links.1, f32[1024,256]{1,0:T(8,128)} %probes.1, ...), custom_call_target="tpu_custom_call" | custom-call | tf_op jit(solution)/shard_map/pallas_call | solution.py:328
  153.7 2.3 %copy.17 = f32[1024,256]{1,0:T(8,128)} copy(f32[1024,256]{1,0:T(8,128)} %get-tuple-element.4) | data formatting | bytes 2097152
  155.9 2.3 %copy.18 = f32[1024,256]{1,0:T(8,128)} copy(f32[1024,256]{1,0:T(8,128)} %get-tuple-element.5) | data formatting | bytes 2097152

commit v2 on v1

--- a/solution.py
+++ b/solution.py
@@ -19,8 +19,10 @@
 CHUNKS = 2
 COLS = PROBES // CHUNKS
 STAGES = 2 * CHUNKS
+AHEAD = 8
 BLOCK = HALF + RANK // 2
 PIECE = BLOCK // 2
+PARTS = 4
 SHARE = PROBES // CHUNKS // PEERS
 
 
@@ -74,7 +76,7 @@
             )
         )
     ]
-    for load in loads:
+    for load in loads[:2]:
         load.start()
 
     barrier = pltpu.get_barrier_semaphore()
@@ -164,11 +166,11 @@
     def product(s, half, slot):
         block = g[s, half, slot, :HALF]
         block = jnp.where(near_has[slot] > 0, block, jnp.zeros_like(block))
-        acc[...] += dot(near_buf[near_slot[slot], :, half * HALF : (half + 1) * HALF], block)
+        acc[s % 2] += dot(near_buf[near_slot[slot], :, half * HALF : (half + 1) * HALF], block)
         block = g[s, half, slot, HALF:]
         block = jnp.where(link_has[slot] > 0, block, jnp.zeros_like(block))
         width = RANK // 2
-        coup[...] += dot(l_bf[link_slot[slot], :, half * width : (half + 1) * width], block)
+        coup[s % 2] += dot(l_bf[link_slot[slot], :, half * width : (half + 1) * width], block)
 
     def make_message(s, v):
         high, low = split(v)
@@ -234,11 +236,13 @@
         far_parent = jnp.concatenate(
             [unfold(far_recv[s, j].astype(F32)) for j in range(PEERS)], axis=0
         ).astype(BF)
-        high, low = split(masked(coup[...] + dot(e_bf[...], far_parent, 1, 1)))
-        return dot_split(u_hi[...], u_lo[...], high, low) + acc[...]
+        high, low = split(masked(coup[s % 2] + dot(e_bf[...], far_parent, 1, 1)))
+        return dot_split(u_hi[...], u_lo[...], high, low) + acc[s % 2]
 
     loads[0].wait()
     loads[1].wait()
+    for load in loads[2:]:
+        load.start()
     u = basis_f[...]
     u_hi[...], u_lo[...] = split(u)
     ut_hi[...], ut_lo[...] = split(u.T)
@@ -261,39 +265,53 @@
     events += [(0, 2), (1, 2), (3, 2), (2, 2)]
     events = [(half, p, q) for p, q in events for half in range(2)]
 
-    @pl.loop(0, STAGES)
-    def _(s):
-        acc[...] = jnp.zeros_like(acc)
-        coup[...] = jnp.zeros_like(coup)
+    def finish(s):
         columns = pl.ds(pl.multiple_of((s % CHUNKS) * COLS, COLS), COLS)
-        for half in range(2):
-            product(s, half, 0)
-        for i, (half, p, q) in enumerate(events):
-            arrive(s, half, p, q)
-            product(s, half, slot_of(half, p, q))
-            if i == 5:
-                pl.when(s == 0)(lambda: parents(0))
-            if i == 9:
-                pl.when(s == 0)(lambda: far(0))
-            if i == 7:
-                pl.when(s + 1 < STAGES)(lambda: parents(s + 1))
-            if i == 15:
-                pl.when(s + 1 < STAGES)(lambda: far(s + 1))
-            if i == 17:
-                pl.when(s + 1 < STAGES)(lambda: send_own(s + 1))
-
         t_buf[s] = combined_result(s)
 
         @pl.when(s < CHUNKS)
         def _():
             pltpu.make_async_copy(t_buf.at[s], out_one.at[:, columns], out_sem.at[s]).start()
-            skeleton = make_message(s + CHUNKS, t_buf[s])
-            upward(s + CHUNKS, skeleton)
+            upward(s + CHUNKS, make_message(s + CHUNKS, t_buf[s]))
 
         @pl.when(s >= CHUNKS)
         def _():
             t_buf[s] = 2.0 * t_buf[s] - v_buf[:, columns]
             pltpu.make_async_copy(t_buf.at[s], out_two.at[:, columns], out_sem.at[s]).start()
+
+    @pl.loop(0, STAGES)
+    def _(s):
+        acc[s % 2] = jnp.zeros((LEAF, COLS), F32)
+        coup[s % 2] = jnp.zeros((RANK, COLS), F32)
+        for half in range(2):
+            product(s, half, 0)
+        for i, (half, p, q) in enumerate(events):
+            if i < AHEAD:
+                pl.when(s == 0)(lambda: arrive(s, half, p, q))
+            else:
+                arrive(s, half, p, q)
+            if i == 11:
+                pl.when(s == 0)(lambda: parents(0))
+            if i == 23:
+                pl.when(s == 0)(lambda: far(0))
+            if i == 23:
+                pl.when(s + 1 < STAGES)(lambda: parents(s + 1))
+            if i == 3:
+                pl.when(s > 0)(lambda: far(s))
+            if i == 13:
+                pl.when(s > 0)(lambda: finish(s - 1))
+            if i == 17:
+                pl.when(s + 1 < STAGES)(lambda: send_own(s + 1))
+            if i == 27:
+
+                @pl.when(s + 1 < STAGES)
+                def _():
+                    for event in events[:AHEAD]:
+                        arrive(s + 1, *event)
+
+            product(s, half, slot_of(half, p, q))
+
+    finish(STAGES - 1)
 
     for s in range(STAGES):
         columns = pl.ds((s % CHUNKS) * COLS, COLS)
@@ -304,6 +322,11 @@
         wait_all(par.at[s, pl.ds(1, rows - 1)], row_ss.at[s])
         wait_all(far_recv.at[s, pl.ds(1, PEERS - 1)], far_ss.at[s])
         pltpu.make_async_copy(t_buf.at[s], out.at[:, columns], out_sem.at[s]).wait()
+
+
+def hand_on(one, two, out_one, out_two):
+    out_one[...] = one[...]
+    out_two[...] = two[...]
 
 
 def local(
@@ -325,7 +348,7 @@
     dma = pltpu.SemaphoreType.DMA
     vmem = pltpu.VMEM
     folded = (2 * SHARE, PARENT // 2)
-    return pl.pallas_call(
+    terms = pl.pallas_call(
         functools.partial(kernel, rows),
         out_shape=[jax.ShapeDtypeStruct((LEAF, PROBES), F32)] * 2,
         in_specs=[smem] * 5 + [hbm] * 6,
@@ -334,8 +357,8 @@
             vmem((STAGES, 2, PEERS, BLOCK, COLS), BF),
             vmem((8, LEAF, LEAF), BF),
             vmem((LEAF, PROBES), F32),
-            vmem((LEAF, COLS), F32),
-            vmem((RANK, COLS), F32),
+            vmem((2, LEAF, COLS), F32),
+            vmem((2, RANK, COLS), F32),
             vmem((STAGES, LEAF, COLS), F32),
             vmem((LEAF, RANK), F32),
             vmem((RANK, PARENT), F32),
@@ -366,6 +389,14 @@
         near_leaves, near_count, leaf_rank, leaf_links, parent_links,
         probes, near_blocks, leaf_basis, leaf_transfer, leaf_link_blocks, parent_link_blocks,
     )
+    part = pl.BlockSpec((LEAF // PARTS, PROBES), lambda i: (i, 0))
+    return pl.pallas_call(
+        hand_on,
+        grid=(PARTS,),
+        out_shape=[jax.ShapeDtypeStruct((LEAF, PROBES), F32)] * 2,
+        in_specs=[part] * 2,
+        out_specs=[part] * 2,
+    )(*terms)
 
 
 def solution(mesh):

time: 158 us -> 140 us (0.89)
  Pallas kernels: 152 us -> 137 us
  local copies, waits for them, and re-layouts: 4.52 us -> 0 us
    pallas_call x1, Pallas kernels: 152 us -> 134 us  [local(): pl.pallas_call(functools.partial(kernel, rows), out_shape=[jax.ShapeDtype...]
    unnamed x2 -> x0, local copies, waits for them, and re-layouts: 4.52 us -> none
    pallas_call x0 -> x1, Pallas kernels: none -> 3.75 us  [local(): pl.pallas_call(hand_on, grid=(PARTS,), out_shape=[jax.ShapeDtypeStruct((L...]
where the time goes in v2:
time: 140 us; the launch traced here: 139 us
  Pallas kernels  137 us (98%)
  between operations  1.93 us (1%)
    pallas_call x1, Pallas kernels, local(): pl.pallas_call(functools.partial(kernel, rows), out_shape=[jax.ShapeDtype...  134 us
    pallas_call x1, Pallas kernels, local(): pl.pallas_call(hand_on, grid=(PARTS,), out_shape=[jax.ShapeDtypeStruct((L...  3.75 us

profile of v2, /device:TPU:0, one launch (start us, length us, event | category | flops | bytes accessed | tf_op | source)
XLA Modules:
  0.0 139.3 jit_solution(12895708034698611507)
XLA Ops:
  1.9 133.6 %shard_map.122 = (f32[1024,256]{1,0:T(8,128)}, f32[1024,256]{1,0:T(8,128)}) custom-call(s32[1,8]{1,0:T(1,128)} %near_leaves.1, s32[1]{0:T(128)S(6)} %copy.13.near_count, s32[1]{0:T(128)S(6)} %copy.14.leaf_rank, s32[1,4]{1,0:T(1,128)} %leaf_links.1, s32[1,2]{1,0:T(1,128)} %parent_links.1, f32[1024,256]{1,0:T(8,128)} %probes.1, ...), custom_call_target="tpu_custom_call" | custom-call | tf_op jit(solution)/shard_map/pallas_call | solution.py:351
  135.6 3.8 %shard_map.123 = (f32[1024,256]{1,0:T(8,128)}, f32[1024,256]{1,0:T(8,128)}) custom-call(f32[1024,256]{1,0:T(8,128)} %get-tuple-element.4.one, f32[1024,256]{1,0:T(8,128)} %get-tuple-element.5.two), custom_call_target="tpu_custom_call" | custom-call | tf_op jit(solution)/shard_map/pallas_call | solution.py:393

commit v3 on v2

--- a/solution.py
+++ b/solution.py
@@ -19,10 +19,10 @@
 CHUNKS = 2
 COLS = PROBES // CHUNKS
 STAGES = 2 * CHUNKS
-AHEAD = 8
+AHEAD = 4
 BLOCK = HALF + RANK // 2
 PIECE = BLOCK // 2
-PARTS = 4
+PARTS = 2
 SHARE = PROBES // CHUNKS // PEERS
 
 
@@ -324,9 +324,25 @@
         pltpu.make_async_copy(t_buf.at[s], out.at[:, columns], out_sem.at[s]).wait()
 
 
-def hand_on(one, two, out_one, out_two):
-    out_one[...] = one[...]
-    out_two[...] = two[...]
+def hand_on(one, two, out_one, out_two, held, sem):
+    rows = LEAF // PARTS
+    steps = []
+    for i, (src, dst) in enumerate(((one, out_one), (two, out_two))):
+        for j in range(PARTS):
+            part = pl.ds(j * rows, rows)
+            steps.append(
+                (
+                    pltpu.make_async_copy(src.at[part], held.at[i, part], sem.at[0, i, j]),
+                    pltpu.make_async_copy(held.at[i, part], dst.at[part], sem.at[1, i, j]),
+                )
+            )
+    for come, _ in steps:
+        come.start()
+    for come, go in steps:
+        come.wait()
+        go.start()
+    for _, go in steps:
+        go.wait()
 
 
 def local(
@@ -389,13 +405,12 @@
         near_leaves, near_count, leaf_rank, leaf_links, parent_links,
         probes, near_blocks, leaf_basis, leaf_transfer, leaf_link_blocks, parent_link_blocks,
     )
-    part = pl.BlockSpec((LEAF // PARTS, PROBES), lambda i: (i, 0))
     return pl.pallas_call(
         hand_on,
-        grid=(PARTS,),
         out_shape=[jax.ShapeDtypeStruct((LEAF, PROBES), F32)] * 2,
-        in_specs=[part] * 2,
-        out_specs=[part] * 2,
+        in_specs=[hbm] * 2,
+        out_specs=[hbm] * 2,
+        scratch_shapes=[vmem((2, LEAF, PROBES), F32), dma((2, 2, PARTS))],
     )(*terms)
 
 

time: 140 us -> 138 us (0.986)
  no operation moved by 1% of the time
where the time goes in v3:
time: 138 us
  Pallas kernels  136 us (99%)
  between operations  2.09 us (2%)
    pallas_call x1, Pallas kernels, local(): pl.pallas_call(functools.partial(kernel, rows), out_shape=[jax.ShapeDtype...  133 us

profile of v3, /device:TPU:0, one launch (start us, length us, event | category | flops | bytes accessed | tf_op | source)
XLA Modules:
  0.0 138.0 jit_solution(5220287732063022294)
XLA Ops:
  1.9 133.5 %shard_map.122 = (f32[1024,256]{1,0:T(8,128)}, f32[1024,256]{1,0:T(8,128)}) custom-call(s32[1,8]{1,0:T(1,128)} %near_leaves.1, s32[1]{0:T(128)S(6)} %copy.13.near_count, s32[1]{0:T(128)S(6)} %copy.14.leaf_rank, s32[1,4]{1,0:T(1,128)} %leaf_links.1, s32[1,2]{1,0:T(1,128)} %parent_links.1, f32[1024,256]{1,0:T(8,128)} %probes.1, ...), custom_call_target="tpu_custom_call" | custom-call | tf_op jit(solution)/shard_map/pallas_call | solution.py:367
  135.4 2.4 %shard_map.123 = (f32[1024,256]{1,0:T(8,128)}, f32[1024,256]{1,0:T(8,128)}) custom-call(f32[1024,256]{1,0:T(8,128)} %get-tuple-element.4.one, f32[1024,256]{1,0:T(8,128)} %get-tuple-element.5.two), custom_call_target="tpu_custom_call" | custom-call | tf_op jit(solution)/shard_map/pallas_call | solution.py:408

commit v4 on v3

--- a/solution.py
+++ b/solution.py
@@ -182,7 +182,7 @@
         return skeleton
 
     def to_peers(src_of, dst_of, ss, rs):
-        for d in range(1, PEERS):
+        for d in (1, 15, 4, 12, 3, 13, 5, 11, 2, 14, 8, 7, 9, 6, 10):
             peer = (me + d) % PEERS
             pltpu.make_async_remote_copy(
                 src_ref=src_of(peer), dst_ref=dst_of(d), send_sem=ss, recv_sem=rs, device_id={"col": peer}

time: 138 us -> 138 us (level)
  no operation moved by 1% of the time
where the time goes in v4:
time: 138 us
  Pallas kernels  136 us (99%)
  between operations  2.09 us (2%)
    pallas_call x1, Pallas kernels, local(): pl.pallas_call(functools.partial(kernel, rows), out_shape=[jax.ShapeDtype...  133 us

profile of v4, /device:TPU:0, one launch (start us, length us, event | category | flops | bytes accessed | tf_op | source)
XLA Modules:
  0.0 137.8 jit_solution(7896437696805188779)
XLA Ops:
  1.9 133.3 %shard_map.122 = (f32[1024,256]{1,0:T(8,128)}, f32[1024,256]{1,0:T(8,128)}) custom-call(s32[1,8]{1,0:T(1,128)} %near_leaves.1, s32[1]{0:T(128)S(6)} %copy.13.near_count, s32[1]{0:T(128)S(6)} %copy.14.leaf_rank, s32[1,4]{1,0:T(1,128)} %leaf_links.1, s32[1,2]{1,0:T(1,128)} %parent_links.1, f32[1024,256]{1,0:T(8,128)} %probes.1, ...), custom_call_target="tpu_custom_call" | custom-call | tf_op jit(solution)/shard_map/pallas_call | solution.py:367
  135.2 2.4 %shard_map.123 = (f32[1024,256]{1,0:T(8,128)}, f32[1024,256]{1,0:T(8,128)}) custom-call(f32[1024,256]{1,0:T(8,128)} %get-tuple-element.4.one, f32[1024,256]{1,0:T(8,128)} %get-tuple-element.5.two), custom_call_target="tpu_custom_call" | custom-call | tf_op jit(solution)/shard_map/pallas_call | solution.py:408
